TPU v7x, 256 devices: a whole 4x4x8 slice. The times are simulated.
256 devices in a mesh: grp: 2 (over core), smp: 8 (over x_lo, y), seq: 16 (over x_hi, z).
Axes of the slice: x: 4 (x_hi: 2, x_lo: 2; x = x_hi * 2 + x_lo), y: 4, z: 8, core: 2. Of those that a mesh axis runs over, the one named last changes fastest.
Arguments:
- resp_q: bfloat16 [16, 2048, 4096], P(('grp', 'smp'), 'seq'), parts along dimension 0, may hold values from -6.5 to 6.5
- resp_kv: bfloat16 [16, 2048, 1024], P(('grp', 'smp'), 'seq'), parts along dimension 0, may hold values from -8 to 8
- prompt_kv: bfloat16 [4096, 1024], P(('grp', 'smp', 'seq')), parts along dimension 0, may hold values from -8 to 8
- resp_len: int32 [16], P(('grp', 'smp')), parts along dimension 0, may hold values from 512 to 2048, as said below
- block_order: int32 [64], P('grp'), parts along dimension 0, may hold values from 0 to 31, each once
- tags: int32 [16, 32], P(('grp', 'smp'), 'seq'), parts along dimension 0, may hold values from 0 to 3
- ver_weight: float32 [4], replicated, may hold values from 0.25 to 2.5
Outputs:
- attended: bfloat16 [16, 2048, 4096], P(('grp', 'smp'), 'seq'), parts along dimension 0
There are 2 independent parts, one for each index of `grp`. A program takes and returns all parts, laid end to end along the dimension named above; an argument that names none is the same for every part. Nothing has to cross between parts.
Inputs may be any that keep to these rules, and one draw needn't show every extreme that they name: `resp_len`: one response in every draw has all 2048 tokens live. `block_order`: each number once.
All inputs are finite; a program needn't handle non-finite values.
Results may differ from a plain program's by a relative error of at most 0.007.
Values may be sent and summed in bfloat16 or wider, within the bound.
A program may use at most 64 MiB of HBM per device.

v0:
```python
import math

import jax
import jax.numpy as jnp
from jax import lax
from jax.sharding import PartitionSpec as P

H = 32
KVH = 4
HD = 128


masked_score = -1e30


def stored_positions(stored, block_order, block_len):
    block_ids = stored // block_len
    matches = block_ids[:, None] == jnp.arange(block_order.shape[0], dtype=jnp.int32)[None, :]
    base = jnp.sum(jnp.where(matches, block_order[None, :], 0), axis=1)
    return base * block_len + stored % block_len


def attend(running, portion, key_pos, queries, query_pos, seq_length, causal):
    count = portion.shape[0]
    block_size = math.gcd(count, 256)
    block_count = count // block_size
    half_width = KVH * HD
    scaling = HD ** (-0.5)
    key_part = portion[:, :half_width].reshape(block_count, block_size, KVH, HD)
    value_part = portion[:, half_width:].reshape(block_count, block_size, KVH, HD)
    pos_part = key_pos.reshape(block_count, block_size)

    def step(current, inputs):
        largest, totals, accum = current
        key_block, value_block, pos_block = inputs
        scores = (
            jnp.einsum("hqd,khd->hqk", queries, key_block, preferred_element_type=jnp.float32)
            * scaling
        )
        if causal:
            allowed = (pos_block[None, :] <= query_pos[:, None]) & (pos_block[None, :] < seq_length)
            scores = jnp.where(allowed[None], scores, masked_score)
        new_largest = jnp.maximum(largest, jnp.max(scores, axis=-1))
        weights = jnp.exp(scores - new_largest[..., None])
        if causal:
            weights = jnp.where(allowed[None], weights, 0.0)
        rescale = jnp.exp(largest - new_largest)
        totals = totals * rescale + jnp.sum(weights, axis=-1)
        accum = accum * rescale[..., None] + jnp.einsum(
            "hqk,khd->hqd",
            weights.astype(jnp.bfloat16),
            value_block,
            preferred_element_type=jnp.float32,
        )
        return ((new_largest, totals, accum), None)

    result, ignored = lax.scan(step, running, (key_part, value_part, pos_part))
    return result


def shards(resp_q, resp_kv, prompt_kv, resp_len, block_order, tags, ver_weight):
    row_count = resp_q.shape[1]
    group_width = H // KVH
    block_len = row_count * lax.axis_size("seq") // block_order.shape[0]
    first_row = lax.axis_index("seq") * row_count
    stored = first_row + jnp.arange(row_count, dtype=jnp.int32)
    query_pos = stored_positions(stored, block_order, block_len)
    seq_length = resp_len[0]
    queries = (
        resp_q[0]
        .reshape(row_count, KVH, group_width, HD)
        .transpose(1, 2, 0, 3)
        .reshape(KVH, group_width * row_count, HD)
    )
    tiled_pos = jnp.tile(query_pos, group_width)
    version_match = tags[0][:, None] == jnp.arange(ver_weight.shape[0], dtype=jnp.int32)[None, :]
    block_weight = jnp.sum(jnp.where(version_match, ver_weight[None, :], 0.0), axis=1)
    row_weight = jnp.where(query_pos < seq_length, jnp.repeat(block_weight, block_len), 0.0)
    start_state = (
        jnp.full((KVH, group_width * row_count), masked_score, jnp.float32),
        jnp.zeros((KVH, group_width * row_count), jnp.float32),
        jnp.zeros((KVH, group_width * row_count, HD), jnp.float32),
    )
    whole_prompt = lax.all_gather(prompt_kv, ("smp", "seq"), axis=0, tiled=True)
    zero_pos = jnp.zeros((whole_prompt.shape[0],), jnp.int32)
    portion = lax.all_gather(resp_kv[0], "seq", axis=0, tiled=True)
    rows_here = jnp.arange(portion.shape[0], dtype=jnp.int32)
    key_pos = stored_positions(rows_here, block_order, block_len)
    final = attend(
        attend(start_state, whole_prompt, zero_pos, queries, tiled_pos, seq_length, False),
        portion,
        key_pos,
        queries,
        tiled_pos,
        seq_length,
        True,
    )
    largest, totals, accum = final
    mixed = accum / totals[..., None]
    mixed = (
        mixed.reshape(KVH, group_width, row_count, HD)
        .transpose(2, 0, 1, 3)
        .reshape(row_count, H * HD)
    )
    return (mixed * row_weight[:, None]).astype(jnp.bfloat16)[None]


def solution(mesh):
    in_specs = (
        P(("grp", "smp"), "seq", None),
        P(("grp", "smp"), "seq", None),
        P(("grp", "smp", "seq"), None),
        P(("grp", "smp")),
        P("grp"),
        P(("grp", "smp"), "seq"),
        P(),
    )
    out_specs = P(("grp", "smp"), "seq", None)
    return jax.shard_map(shards, mesh=mesh, in_specs=in_specs, out_specs=out_specs, check_vma=False)
```

profile of v0, /device:TPU:0, one launch (start us, length us, event | category | flops | bytes accessed | tf_op | source)
XLA Modules:
  0.0 919.6 jit_solution(8655499721212162130)
XLA Ops:
  8.1 1.5 copy.50
  11.3 99.9 %all-gather.6.cloned.1.call-done = bf16[1,2048,1024]{2,1,0:T(8,128)(2,1)} async-done(((bf16[1,128,1024]{2,1,0:T(8,128)(2,1)}), bf16[1,2048,1024]{2,1,0:T(8,128)(2,1)}) %all-gather.6.cloned.1.call-update) | async-done | bytes 4194320 | tf_op jit(solution)/shard_map/all_gather | solution.py:86
  111.2 4.5 fusion.39
  115.7 4.0 reshape.202
  119.6 4.0 reshape.203
  123.6 643.9 %all-gather.4.cloned.1.call-done = bf16[2048,1024]{1,0:T(8,128)(2,1)} async-done(((bf16[16,1024]{1,0:T(8,128)(2,1)}), bf16[2048,1024]{1,0:T(8,128)(2,1)}) %all-gather.4.cloned.1.call-update) | async-done | bytes 4194320 | tf_op jit(solution)/shard_map/all_gather | solution.py:84
  767.5 4.5 fusion.40
  771.9 4.0 reshape.200
  775.9 4.0 reshape.201
  779.9 74.0 %while.31 = (s32[]{:T(128)}, f32[4,1024]{1,0:T(4,128)S(1)}, f32[4,1024]{1,0:T(4,128)S(1)}, f32[4,1024,128]{2,1,0:T(8,128)S(1)}, bf16[8,256,4,128]{3,2,1,0:T(4,12...) while((s32[]{:T(128)}, f32[4,1024]{1,0:T(4,128)S(1)}, ...), condition=%wide.region_3.4_spmd.clone, body=%wide.region_0.3_spmd.clone.sunk | while | flops 546852864 | bytes 36438152 | solution.py:57
  781.1 2.7 bitcast_reduce_fusion.2
  783.8 3.1 fusion.58
  787.3 1.8 fusion.60
  790.4 2.7 bitcast_reduce_fusion.2
  793.1 3.1 fusion.58
  796.5 1.8 fusion.60
  799.6 2.7 bitcast_reduce_fusion.2
  802.3 3.1 fusion.58
  805.8 1.8 fusion.60
  808.9 2.7 bitcast_reduce_fusion.2
  811.6 3.1 fusion.58
  815.0 1.8 fusion.60
  818.1 2.7 bitcast_reduce_fusion.2
  820.8 3.1 fusion.58
  824.3 1.8 fusion.60
  827.4 2.7 bitcast_reduce_fusion.2
  830.1 3.1 fusion.58
  833.5 1.8 fusion.60
  836.6 2.7 bitcast_reduce_fusion.2
  839.4 3.1 fusion.58
  842.8 1.8 fusion.60
  845.9 2.7 bitcast_reduce_fusion.2
  848.6 3.1 fusion.58
  852.0 1.8 fusion.60
  853.9 52.5 %while.30 = (s32[]{:T(128)}, f32[4,1024]{1,0:T(4,128)S(1)}, f32[4,1024]{1,0:T(4,128)S(1)}, f32[4,1024,128]{2,1,0:T(8,128)S(1)}, s32[8,256]{1,0:T(8,128)S(1)}, /*...) while((s32[]{:T(128)}, f32[4,1024]{1,0:T(4,128)S(1)}, ...), condition=%wide.region_9.10_spmd.clone, body=%wide.region_6.9_spmd.clone.sunk | while | flops 552083712 | bytes 20721784 | solution.py:57
  858.2 2.3 multiply_add_fusion.5
  861.4 1.2 constant_dynamic-slice_fusion.8
  864.7 2.3 multiply_add_fusion.5
  871.3 2.3 multiply_add_fusion.5
  877.9 2.3 multiply_add_fusion.5
  884.5 2.3 multiply_add_fusion.5
  887.7 1.2 constant_dynamic-slice_fusion.8
  891.0 2.3 multiply_add_fusion.5
  894.3 1.2 constant_dynamic-slice_fusion.8
  897.6 2.3 multiply_add_fusion.5
  904.2 2.3 multiply_add_fusion.5
  907.2 2.6 copy.64
  909.8 1.7 reshape.197
  (144 shorter events, 47.2 us)
Async XLA Ops:
  6.5 104.7 %all-gather.6.cloned.1.call-start = ((), (), s32[]{:S(2)}) async-start(), calls=%async_computation.1 | async-start | bytes 4456448 | tf_op jit(solution)/shard_map/all_gather | solution.py:86
  7.3 760.2 %all-gather.4.cloned.1.call-start = ((), (), s32[]{:S(2)}) async-start(), calls=%async_computation | async-start | bytes 4227072 | tf_op jit(solution)/shard_map/all_gather | solution.py:84
  8.0 1.9 copy-start.2
  8.0 1.9 copy-start.3
  8.1 2.9 copy-start.1
  783.8 3.5 copy-start
  793.1 3.5 copy-start
  802.3 3.5 copy-start
  811.6 3.5 copy-start
  820.8 3.5 copy-start
  830.1 3.5 copy-start
  839.3 3.5 copy-start
  848.6 3.5 copy-start
Sparse Core Ops, SparseCore 0:
  9.9 101.2 all-gather.5
  113.0 654.4 all-gather.3
where the time goes:
time: 920 us
  waiting for transfers between devices  745 us (81%)
  matrix products  62.6 us (7%)
  local copies, waits for them, and re-layouts  53.5 us (6%)
  other arithmetic  43.1 us (5%)
  between operations  14.2 us (2%)
    all_gather x1, waiting for transfers between devices, shards(): whole_prompt = lax.all_gather(prompt_kv, ('smp', 'seq'), axis=0, tiled=True)  644 us
    all_gather x1, waiting for transfers between devices, shards(): portion = lax.all_gather(resp_kv[0], 'seq', axis=0, tiled=True)  99.9 us
    dot_general x16, matrix products, step(): jnp.einsum('hqk,khd->hqd', weights.astype(jnp.bfloat16), value_block, pre...  33.2 us
    reduce_sum x16, other arithmetic, step(): totals = totals * rescale + jnp.sum(weights, axis=-1)  32.9 us
    dot_general x16, matrix products, step(): jnp.einsum('hqd,khd->hqk', queries, key_block, preferred_element_type=jnp...  29.4 us
    dynamic_slice x16, local copies, waits for them, and re-layouts, attend(): result, ignored = lax.scan(step, running, (key_part, value_part, pos_part))  19.5 us
  transfers between devices with their start and end apart: 2, of which 2 were waited for; matrix products, arithmetic and copies ran while one was open for 2% of the time, Pallas kernels for 0%

commit v1 on v0

v1 whole, which is shorter than its diff:
```python
import functools
import math

import jax
import jax.numpy as jnp
from jax import lax
from jax.experimental import pallas as pl
from jax.experimental.pallas import tpu as pltpu
from jax.sharding import PartitionSpec as P

MESH = pl.DeviceIdType.MESH
F32 = jnp.float32
BF16 = jnp.bfloat16
H = 32
KVH = 4
HD = 128
GW = H // KVH
HALF = KVH * HD
ROWS = 128
BLK = 64
NX, NY, NZ = 4, 4, 8
NPB = NX * NY
SCALE = HD**-0.5 * math.log2(math.e)
LEAST, MOST = 2.0**-80, 2.0**100

M_EXCH = 0
M_PIECE = 1
M_Z = M_PIECE + NZ - 1
M_X = M_Z + 16
M_Y = M_X + 4
N_MSG = M_Y + 16


def positions(order_ref, block, along, shape):
    index = lax.broadcasted_iota(jnp.int32, shape, along)
    first, second = order_ref[2 * block], order_ref[2 * block + 1]
    return jnp.where(index < BLK, first * BLK + index, second * BLK + index - BLK)


def row_scale(order_ref, len_ref, tags_ref, weight_ref, seq):
    shape = (1, ROWS)
    query_pos = positions(order_ref, seq, 1, shape)
    picked = []
    for k in range(2):
        value = jnp.float32(0.0)
        for v in range(weight_ref.shape[0]):
            value = jnp.where(tags_ref[0, k] == v, weight_ref[v], value)
        picked.append(value)
    index = lax.broadcasted_iota(jnp.int32, shape, 1)
    weight = jnp.where(index < BLK, picked[0], picked[1])
    return jnp.where(query_pos < len_ref[0], weight, 0.0)


def block_bias(order_ref, len_ref, seq, block):
    shape = (ROWS, ROWS)
    query_pos = positions(order_ref, seq, 1, shape)
    key_pos = positions(order_ref, block, 0, shape)
    allowed = (key_pos <= query_pos) & (key_pos < len_ref[0])
    return jnp.where(allowed, 0.0, -jnp.inf).astype(F32)


def gather_attend(
    len_ref, order_ref, tags_ref, weight_ref, q_ref, own_ref, piece_ref,
    out_ref, bad_ref, kept_ref,
    kv, qa, acc, bias, send_sem, recv_sem, keep_sem,
):
    grp, smp, seq = lax.axis_index("grp"), lax.axis_index("smp"), lax.axis_index("seq")
    x_hi, z = lax.div(seq, NZ), lax.rem(seq, NZ)
    x_lo, y = lax.div(smp, NY), lax.rem(smp, NY)
    x = x_hi * 2 + x_lo

    def device(dx, dy, dz):
        xx, yy, zz = lax.rem(x + dx + NX, NX), lax.rem(y + dy + NY, NY), lax.rem(z + dz + NZ, NZ)
        return (grp, lax.rem(xx, 2) * NY + yy, lax.div(xx, 2) * NZ + zz)

    def rblock(lane, dz):
        column = x_hi if lane == 0 else 1 - x_hi
        return NPB + column * NZ + lax.rem(z + dz + NZ, NZ)

    def pblock(dx, dy):
        return lax.rem(x + dx + NX, NX) * NY + lax.rem(y + dy + NY, NY)

    peers = [device(0, 0, d) for d in range(1, NZ)]
    peers += [device(d, 0, 0) for d in range(1, NX)] + [device(0, 1, 0), device(0, -1, 0)]
    barrier = pltpu.get_barrier_semaphore()
    for peer in peers:
        pl.semaphore_signal(barrier, inc=1, device_id=peer, device_id_type=MESH)

    def copy(message, src, dst, to):
        return pltpu.make_async_remote_copy(
            src_ref=src, dst_ref=dst, send_sem=send_sem.at[message], recv_sem=recv_sem.at[message],
            device_id=to, device_id_type=MESH,
        )

    parts = {"all": (0, ROWS), "low": (0, ROWS // 2), "high": (ROWS // 2, ROWS // 2)}
    started = {}

    def part_of(block, part):
        start, size = parts[part]
        return kv.at[block, pl.ds(start, size), :]

    def send(message, block, part, to, src=None):
        there = part_of(block, part)
        started[message] = part
        copy(message, there if src is None else src, there, to).start()

    def arrive(message, block, part="all"):
        here = part_of(block, part)
        copy(message, here, here, device(0, 0, 1)).wait_recv()

    for h in range(KVH):
        for g in range(GW):
            column = (h * GW + g) * HD
            scaled = q_ref[:, column : column + HD].T.astype(F32) * SCALE
            high = scaled.astype(BF16)
            qa[h, 0:HD, g * ROWS : (g + 1) * ROWS] = high
            qa[h, HD : 2 * HD, g * ROWS : (g + 1) * ROWS] = (scaled - high.astype(F32)).astype(BF16)
    own_block, own_prompt = rblock(0, 0), pblock(0, 0)
    kv[own_block] = own_ref[...]
    kv[own_prompt, pl.ds(pl.multiple_of(z * 16, 16), 16), :] = piece_ref[...]

    pl.semaphore_wait(barrier, len(peers))

    mine = kv.at[own_prompt, pl.ds(pl.multiple_of(z * 16, 16), 16), :]
    for d in (1, 7, 2, 6, 3, 5, 4):
        copy(M_PIECE + d - 1, piece_ref, mine, device(0, 0, d)).start()
    copy(M_EXCH, own_ref, kv.at[own_block], device(2, 0, 0)).start()
    started[M_EXCH] = "all"

    def z_step(lane, step):
        base = M_Z + lane * 8 + (step - 1) * 2
        low, high = ("low", "high") if step == NZ // 2 else ("all", "all")
        send(base, rblock(lane, 1 - step), low, device(0, 0, 1))
        send(base + 1, rblock(lane, step - 1), high, device(0, 0, -1))

    def z_arrive(lane, step):
        base = M_Z + lane * 8 + (step - 1) * 2
        low, high = ("low", "high") if step == NZ // 2 else ("all", "all")
        arrive(base, rblock(lane, -step), low)
        arrive(base + 1, rblock(lane, step), high)

    def x_step(step):
        base = M_X + (step - 1) * 2
        low, high = ("low", "high") if step == 2 else ("all", "all")
        send(base, pblock(1 - step, 0), low, device(1, 0, 0))
        send(base + 1, pblock(step - 1, 0), high, device(-1, 0, 0))

    def x_arrive(step):
        base = M_X + (step - 1) * 2
        low, high = ("low", "high") if step == 2 else ("all", "all")
        arrive(base, pblock(-step, 0), low)
        arrive(base + 1, pblock(step, 0), high)

    def y_step(dx, step):
        base = M_Y + (dx % NX) * 4 + (step - 1) * 2
        low, high = ("low", "high") if step == 2 else ("all", "all")
        send(base, pblock(dx, 1 - step), low, device(0, 1, 0))
        send(base + 1, pblock(dx, step - 1), high, device(0, -1, 0))

    def y_arrive(dx, step):
        base = M_Y + (dx % NX) * 4 + (step - 1) * 2
        low, high = ("low", "high") if step == 2 else ("all", "all")
        arrive(base, pblock(dx, -step), low)
        arrive(base + 1, pblock(dx, step), high)

    z_step(0, 1)

    bias[0] = jnp.zeros((ROWS, ROWS), F32)

    def set_bias(block, _):
        bias[block + 1] = block_bias(order_ref, len_ref, seq, block)
        return 0

    lax.fori_loop(0, 2 * NZ, set_bias, 0)
    acc[...] = jnp.zeros_like(acc)

    def event_0():
        for d in range(1, NZ):
            there = kv.at[own_prompt, pl.ds(pl.multiple_of(lax.rem(z - d + NZ, NZ) * 16, 16), 16), :]
            copy(M_PIECE + d - 1, there, there, device(0, 0, 1)).wait_recv()
        y_step(0, 1)
        x_step(1)

    def event_1():
        arrive(M_EXCH, rblock(1, 0))
        z_step(1, 1)
        z_arrive(0, 1)
        z_step(0, 2)

    def event_2():
        y_arrive(0, 1)
        y_step(0, 2)
        x_arrive(1)
        x_step(2)
        y_step(1, 1)
        y_step(-1, 1)

    def event_3():
        y_arrive(0, 2)

    def event_4():
        z_arrive(1, 1)
        z_step(1, 2)

    def event_5():
        x_arrive(2)
        y_step(2, 1)

    def event_6():
        z_arrive(0, 2)
        z_step(0, 3)

    def event_7():
        y_arrive(1, 1)
        y_step(1, 2)

    def event_8():
        z_arrive(1, 2)
        z_step(1, 3)

    def event_9():
        y_arrive(-1, 1)
        y_step(-1, 2)

    def event_10():
        z_arrive(0, 3)
        z_step(0, 4)

    def event_11():
        y_arrive(1, 2)
        y_arrive(-1, 2)

    def event_12():
        y_arrive(2, 1)
        y_step(2, 2)

    def event_13():
        z_arrive(1, 3)
        z_step(1, 4)

    def event_14():
        y_arrive(2, 2)

    def event_15():
        z_arrive(0, 4)
        z_arrive(1, 4)

    units = [
        (event_0, own_block, own_prompt),
        (event_1, rblock(0, -1), rblock(0, 1)),
        (event_2, pblock(0, -1), pblock(0, 1)),
        (event_3, rblock(1, 0), pblock(0, 2)),
        (event_4, rblock(1, -1), rblock(1, 1)),
        (event_5, pblock(1, 0), pblock(-1, 0)),
        (event_6, rblock(0, -2), rblock(0, 2)),
        (event_7, pblock(1, -1), pblock(1, 1)),
        (event_8, rblock(1, -2), rblock(1, 2)),
        (event_9, pblock(-1, -1), pblock(-1, 1)),
        (event_10, rblock(0, -3), rblock(0, 3)),
        (event_11, pblock(1, 2), pblock(-1, 2)),
        (event_12, pblock(2, -1), pblock(2, 1)),
        (event_13, rblock(1, -3), rblock(1, 3)),
        (event_14, pblock(2, 0), pblock(2, 2)),
        (event_15, rblock(0, 4), rblock(1, 4)),
    ]
    ones = jnp.ones((16, 2 * ROWS), BF16)

    def keep(unit, block, which):
        return pltpu.make_async_copy(kv.at[block], kept_ref.at[block], keep_sem.at[2 * unit + which])

    def pick(t, which):
        block = units[0][which]
        for i, unit in enumerate(units):
            block = jnp.where(t == i, unit[which], block)
        return block

    def work(t, _):
        for i, unit in enumerate(units):
            pl.when(t == i)(unit[0])
        one, two = pick(t, 1), pick(t, 2)
        keep(t, one, 0).start()
        keep(t, two, 1).start()
        bias_one = bias.at[jnp.maximum(one - (NPB - 1), 0)]
        bias_two = bias.at[jnp.maximum(two - (NPB - 1), 0)]

        def scores(h):
            k = jnp.concatenate(
                [kv[one, :, h * HD : (h + 1) * HD], kv[two, :, h * HD : (h + 1) * HD]], axis=0
            )
            return jnp.dot(jnp.concatenate([k, k], axis=1), qa[h], preferred_element_type=F32)

        def weights(s):
            b = jnp.concatenate([bias_one[...], bias_two[...]], axis=0)
            s = jnp.concatenate([s[:, g * ROWS : (g + 1) * ROWS] + b for g in range(GW)], axis=1)
            return jnp.exp2(s).astype(BF16)

        def mix(h, p):
            column = HALF + h * HD
            v = jnp.concatenate(
                [kv[one, :, column : column + HD].T, kv[two, :, column : column + HD].T], axis=1
            )
            acc[h] += jnp.dot(jnp.concatenate([v, ones], axis=0), p, preferred_element_type=F32)

        s, p = {0: scores(0)}, {}
        for h in range(KVH + 1):
            if h + 1 < KVH:
                s[h + 1] = scores(h + 1)
            if h >= 1:
                mix(h - 1, p.pop(h - 1))
            if h < KVH:
                p[h] = weights(s.pop(h))
        return 0

    lax.fori_loop(0, len(units), work, 0)

    scale_row = row_scale(order_ref, len_ref, tags_ref, weight_ref, seq)
    bad = jnp.zeros((1, ROWS), F32)
    for h in range(KVH):
        for g in range(GW):
            columns = slice(g * ROWS, (g + 1) * ROWS)
            total = acc[h, HD : HD + 1, columns]
            bad = jnp.where((total >= LEAST) & (total <= MOST), bad, 1.0)
            mixed = (acc[h, 0:HD, columns] * (scale_row / total)).astype(BF16)
            column = (h * GW + g) * HD
            out_ref[:, column : column + HD] = mixed.T
    bad_ref[...] = bad

    for t, unit in enumerate(units):
        keep(t, unit[1], 0).wait()
        keep(t, unit[2], 1).wait()
    for d in range(1, NZ):
        copy(M_PIECE + d - 1, piece_ref, mine, device(0, 0, d)).wait_send()
    for message, part in started.items():
        here = part_of(own_block, part)
        copy(message, here, here, device(0, 0, 1)).wait_send()


def check_rows(len_ref, order_ref, tags_ref, weight_ref, bad_ref, q_ref, kept_ref, first_ref, out_ref, q, kv, out, sem):
    del first_ref
    seq = lax.axis_index("seq")

    @pl.when(jnp.max(bad_ref[...]) > 0.0)
    def redo():
        for src, dst in ((q_ref, q), (kept_ref, kv)):
            fetch = pltpu.make_async_copy(src, dst, sem)
            fetch.start()
            fetch.wait()
        scale_row = row_scale(order_ref, len_ref, tags_ref, weight_ref, seq)

        def head(index, _):
            columns = pl.ds(pl.multiple_of(index * HD, HD), HD)
            kv_head = lax.div(index, GW)
            key_columns = pl.ds(pl.multiple_of(kv_head * HD, HD), HD)
            value_columns = pl.ds(pl.multiple_of(HALF + kv_head * HD, HD), HD)
            queries = q[:, columns]

            def scores(block):
                s = lax.dot_general(
                    kv[block, :, key_columns], queries, (((1,), (1,)), ((), ())), preferred_element_type=F32
                )
                b = block_bias(order_ref, len_ref, seq, jnp.maximum(block - NPB, 0))
                return jnp.where(block < NPB, s * SCALE, s * SCALE + b)

            def top_of(block, top):
                return jnp.maximum(top, jnp.max(scores(block), axis=0, keepdims=True))

            blocks = kv.shape[0]
            top = lax.fori_loop(0, blocks, top_of, jnp.full((1, ROWS), -jnp.inf, F32))

            def add(block, carry):
                total, mixed = carry
                w = jnp.exp2(scores(block) - top)
                total += jnp.sum(w, axis=0, keepdims=True)
                mixed += jnp.dot(kv[block, :, value_columns].T, w.astype(BF16), preferred_element_type=F32)
                return total, mixed

            total, mixed = lax.fori_loop(
                0, blocks, add, (jnp.zeros((1, ROWS), F32), jnp.zeros((HD, ROWS), F32))
            )
            out[:, columns] = (mixed * (scale_row / total)).astype(BF16).T
            return 0

        lax.fori_loop(0, H, head, 0)
        store = pltpu.make_async_copy(out, out_ref, sem)
        store.start()
        store.wait()


def shards(resp_q, resp_kv, prompt_kv, resp_len, block_order, tags, ver_weight):
    blocks = NPB + 2 * NZ
    smem = pl.BlockSpec(memory_space=pltpu.SMEM)
    vmem = pl.BlockSpec(memory_space=pltpu.VMEM)
    anywhere = pl.BlockSpec(memory_space=pl.ANY)
    scalars = (resp_len, block_order, tags, ver_weight)
    queries = resp_q[0]
    width = 2 * HALF
    keys = blocks * ROWS
    attended, bad, kept = pl.pallas_call(
        gather_attend,
        out_shape=(
            jax.ShapeDtypeStruct((ROWS, H * HD), BF16),
            jax.ShapeDtypeStruct((1, ROWS), F32),
            jax.ShapeDtypeStruct((blocks, ROWS, width), BF16),
        ),
        in_specs=[smem] * 4 + [vmem] * 3,
        out_specs=(vmem, vmem, anywhere),
        scratch_shapes=[
            pltpu.VMEM((blocks, ROWS, width), BF16),
            pltpu.VMEM((KVH, 2 * HD, GW * ROWS), BF16),
            pltpu.VMEM((KVH, HD + 16, GW * ROWS), F32),
            pltpu.VMEM((2 * NZ + 1, ROWS, ROWS), F32),
            pltpu.SemaphoreType.DMA((N_MSG,)),
            pltpu.SemaphoreType.DMA((N_MSG,)),
            pltpu.SemaphoreType.DMA((blocks,)),
        ],
        compiler_params=pltpu.CompilerParams(
            collective_id=0, has_side_effects=True, vmem_limit_bytes=48 * 2**20
        ),
        cost_estimate=pl.CostEstimate(
            flops=4 * ROWS * H * HD * keys, bytes_accessed=2 * keys * width, transcendentals=ROWS * H * keys
        ),
    )(*scalars, queries, resp_kv[0], prompt_kv)
    final = pl.pallas_call(
        check_rows,
        out_shape=jax.ShapeDtypeStruct((ROWS, H * HD), BF16),
        in_specs=[smem] * 4 + [vmem] + [anywhere] * 3,
        out_specs=anywhere,
        scratch_shapes=[
            pltpu.VMEM((ROWS, H * HD), BF16),
            pltpu.VMEM((blocks, ROWS, width), BF16),
            pltpu.VMEM((ROWS, H * HD), BF16),
            pltpu.SemaphoreType.DMA,
        ],
        input_output_aliases={7: 0},
        compiler_params=pltpu.CompilerParams(vmem_limit_bytes=32 * 2**20),
    )(*scalars, bad, queries, kept, attended)
    return final[None]


def solution(mesh):
    in_specs = (
        P(("grp", "smp"), "seq", None),
        P(("grp", "smp"), "seq", None),
        P(("grp", "smp", "seq"), None),
        P(("grp", "smp")),
        P("grp"),
        P(("grp", "smp"), "seq"),
        P(),
    )
    out_specs = P(("grp", "smp"), "seq", None)
    return jax.shard_map(shards, mesh=mesh, in_specs=in_specs, out_specs=out_specs, check_vma=False)
```

time: 920 us -> 566 us (0.62)
  waiting for transfers between devices: 745 us -> 0 us
  Pallas kernels: 0 us -> 554 us
  matrix products: 62.6 us -> 0 us
  local copies, waits for them, and re-layouts: 53.5 us -> 9.24 us
  other arithmetic: 43.1 us -> 0 us
  between operations: 14.2 us -> 0.69 us
    all_gather x2 -> x0, waiting for transfers between devices: 744 us -> none  [the longest x1 644 us: shards(): whole_prompt = lax.all_gather(prompt_kv, ('smp', 'seq'), axis=0, tiled=True)]
    pallas_call x0 -> x2, Pallas kernels: none -> 554 us  [the longest x1 496 us: shards(): pl.pallas_call(check_rows, out_shape=jax.ShapeDtypeStruct((ROWS, H * HD),...]
    dot_general x32 -> x0, matrix products: 62.6 us -> none  [the longest x16 33.2 us: step(): jnp.einsum('hqk,khd->hqd', weights.astype(jnp.bfloat16), value_block, pre...]
    reduce_sum x19 -> x0, other arithmetic: 33.3 us -> none  [the longest x16 32.9 us: step(): totals = totals * rescale + jnp.sum(weights, axis=-1)]
    reshape x7 -> x0, local copies, waits for them, and re-layouts: 20.3 us -> none  [the longest x2 7.96 us: attend(): portion[:, half_width:].reshape(block_count, block_size, KVH, HD)]
    dynamic_slice x16 -> x0, local copies, waits for them, and re-layouts: 19.5 us -> none  [attend(): result, ignored = lax.scan(step, running, (key_part, value_part, pos_part))]
  transfers between devices with their start and end apart: 2 -> 0, of which waited for: 2 -> 0; matrix products, arithmetic and copies ran while one was open for 2% -> 0% of each run, Pallas kernels for 0% -> 0%
where the time goes in v1:
time: 566 us; the launch traced here: 564 us
  Pallas kernels  554 us (98%)
  local copies, waits for them, and re-layouts  9.24 us (2%)
    pallas_call x1, Pallas kernels, shards(): pl.pallas_call(check_rows, out_shape=jax.ShapeDtypeStruct((ROWS, H * HD),...  496 us
    pallas_call x1, Pallas kernels, shards(): pl.pallas_call(gather_attend, out_shape=(jax.ShapeDtypeStruct((ROWS, H *...  58.5 us

profile of v1, /device:TPU:0, one launch (start us, length us, event | category | flops | bytes accessed | tf_op | source)
XLA Modules:
  0.0 564.4 jit_solution(17575388690362997664)
XLA Ops:
  0.7 0.0 copy-start.1
  0.7 1.2 copy-done.1
  1.9 0.0 copy-start.2
  1.9 0.7 copy-done.2
  2.5 0.0 copy-start.3
  2.5 0.7 copy-done.3
  3.2 0.0 copy-start.4
  3.2 0.7 copy-done.4
  3.8 0.0 copy-start.5
  3.8 0.9 copy-done.5
  4.8 0.0 copy-start.6
  4.8 0.8 copy-done.6
  5.6 58.5 %shard_map.73 = (bf16[128,4096]{1,0:T(8,128)(2,1)S(1)}, f32[1,128]{1,0:T(1,128)S(1)}, bf16[32,128,1024]{2,1,0:T(8,128)(2,1)}) custom-call(s32[1]{0:T(128)S(6)} %copy.11.len_ref, s32[32]{0:T(128)S(1)} %copy-done.2, s32[1,2]{1,0:T(1,128)S(1)} %copy-done.3, f32[4]{0:T(128)S(1)} %copy-done.4, bf16[128,4096]{1,0:T(8,128)(2,1)S(1)} %bitcast.4, ...), custom_call_target="tpu_custom_call" | custom-call | flops 8589934592 | bytes 8388608 | tf_op jit(solution)/shard_map/pallas_call | solution.py:398
  64.1 0.0 copy-start
  64.1 3.4 copy-done
  67.5 495.9 %shard_map.74 = bf16[128,4096]{1,0:T(8,128)(2,1)S(1)} custom-call(s32[1]{0:T(128)S(6)} %copy.11.len_ref, s32[32]{0:T(128)S(1)} %copy-done.2, s32[1,2]{1,0:T(1,128)S(1)} %copy-done.3, f32[4]{0:T(128)S(1)} %copy-done.4, f32[1,128]{1,0:T(1,128)S(1)} %get-tuple-element.8.bad_ref, bf16[128,4096]{1,0:T(8,128)(2,1)S(1)} %bitcast.5, ...), custom_call_target="tpu_custom_call", output_to_operand_aliasing={{}: (7, {})} | custom-call | tf_op jit(solution)/shard_map/pallas_call | solution.py:423
  563.4 1.0 copy.12
Async XLA Ops:
  0.7 1.2 copy-start.1
  1.9 0.7 copy-start.2
  2.5 0.7 copy-start.3
  3.2 0.7 copy-start.4
  3.8 0.9 copy-start.5
  4.8 0.8 copy-start.6
  64.1 3.4 copy-start

commit v2 on v1

v2 whole, which is shorter than its diff:
```python
import functools
import math

import jax
import jax.numpy as jnp
from jax import lax
from jax.experimental import pallas as pl
from jax.experimental.pallas import tpu as pltpu
from jax.sharding import PartitionSpec as P

MESH = pl.DeviceIdType.MESH
F32 = jnp.float32
BF16 = jnp.bfloat16
H = 32
KVH = 4
HD = 128
GW = H // KVH
HALF = KVH * HD
ROWS = 128
BLK = 64
NX, NY, NZ = 4, 4, 8
NPB = NX * NY
SCALE = HD**-0.5 * math.log2(math.e)
LEAST, MOST = 2.0**-80, 2.0**100

PIECE = 16
PART = 256
WHOLE, FEW, MOST_OF = slice(0, 4), slice(0, 1), slice(1, 4)
KINDS = {"few": (FEW, 0), "own": (MOST_OF, 0), "other": (MOST_OF, 1)}
ALL, LOW, HIGH = (0, ROWS), (0, ROWS // 2), (ROWS // 2, ROWS // 2)
NEAR, FAR = (0, 5 * PIECE), (5 * PIECE, 3 * PIECE)
N_MSG = 64
PARTS = 4


def positions(order_ref, block, along, shape):
    index = lax.broadcasted_iota(jnp.int32, shape, along)
    first, second = order_ref[2 * block], order_ref[2 * block + 1]
    return jnp.where(index < BLK, first * BLK + index, second * BLK + index - BLK)


def row_scale(order_ref, len_ref, tags_ref, weight_ref, seq):
    shape = (1, ROWS)
    query_pos = positions(order_ref, seq, 1, shape)
    picked = []
    for k in range(2):
        value = jnp.float32(0.0)
        for v in range(weight_ref.shape[0]):
            value = jnp.where(tags_ref[0, k] == v, weight_ref[v], value)
        picked.append(value)
    index = lax.broadcasted_iota(jnp.int32, shape, 1)
    weight = jnp.where(index < BLK, picked[0], picked[1])
    return jnp.where(query_pos < len_ref[0], weight, 0.0)


def block_bias(order_ref, len_ref, seq, block):
    shape = (ROWS, ROWS)
    query_pos = positions(order_ref, seq, 1, shape)
    key_pos = positions(order_ref, block, 0, shape)
    allowed = (key_pos <= query_pos) & (key_pos < len_ref[0])
    return jnp.where(allowed, 0.0, -jnp.inf).astype(F32)


def gather_attend(
    len_in, order_in, tags_in, weight_in, q_in, own_in, piece_in,
    out_ref, bad_ref, kept_ref,
    len_ref, order_ref, tags_ref, weight_ref, q_ref,
    kv, qa, acc, bias, load_sem, send_sem, recv_sem, keep_sem,
):
    grp, smp, seq = lax.axis_index("grp"), lax.axis_index("smp"), lax.axis_index("seq")
    x_hi, z = lax.div(seq, NZ), lax.rem(seq, NZ)
    x_lo, y = lax.div(smp, NY), lax.rem(smp, NY)
    x = x_hi * 2 + x_lo

    def device(dx, dy, dz):
        xx, yy, zz = lax.rem(x + dx + NX, NX), lax.rem(y + dy + NY, NY), lax.rem(z + dz + NZ, NZ)
        return (grp, lax.rem(xx, 2) * NY + yy, lax.div(xx, 2) * NZ + zz)

    def rblock(lane, dz):
        column = x_hi if lane == 0 else 1 - x_hi
        return NPB + column * NZ + lax.rem(z + dz + NZ, NZ)

    def pblock(dx, dy):
        return lax.rem(x + dx + NX, NX) * NY + lax.rem(y + dy + NY, NY)

    peers = [device(0, 0, d) for d in range(1, NZ)]
    peers += [device(d, 0, 0) for d in range(1, NX)] + [device(0, 1, 0), device(0, -1, 0)]
    barrier = pltpu.get_barrier_semaphore()
    for peer in peers:
        pl.semaphore_signal(barrier, inc=1, device_id=peer, device_id_type=MESH)

    own_block, own_prompt = rblock(0, 0), pblock(0, 0)
    pairs = [(piece_in.at[:, k * PART : (k + 1) * PART], kv.at[k, own_prompt, 0:PIECE, :]) for k in range(4)]
    pairs += [(own_in.at[:, k * PART : (k + 1) * PART], kv.at[k, own_block]) for k in range(4)]
    pairs += [(q_in, q_ref), (len_in, len_ref), (order_in, order_ref), (tags_in, tags_ref), (weight_in, weight_ref)]
    loads = [pltpu.make_async_copy(src, dst, load_sem.at[i]) for i, (src, dst) in enumerate(pairs)]
    for load in loads:
        load.start()

    sent = {}
    numbers = {}

    def number(name):
        return numbers.setdefault(name, len(numbers))

    def piece_of(which, block, rows):
        start, size = rows
        return kv.at[which, block, pl.ds(start, size), :]

    def copy(name, ref, to):
        m = number(name)
        return pltpu.make_async_remote_copy(
            src_ref=ref[0], dst_ref=ref[1], send_sem=send_sem.at[m], recv_sem=recv_sem.at[m],
            device_id=to, device_id_type=MESH,
        )

    def send(name, which, block, rows, to, there=None):
        src = piece_of(which, block, rows)
        dst = src if there is None else piece_of(which, block, there)
        sent[name] = (which, rows)
        copy(name, (src, dst), to).start()

    def arrive(name, which, block, rows=ALL):
        here = piece_of(which, block, rows)
        copy(name, (here, here), device(0, 0, 1)).wait_recv()

    def z_step(kind, step):
        which, lane = KINDS[kind]
        low, high = (LOW, HIGH) if step == NZ // 2 else (ALL, ALL)
        send((kind, step, 1), which, rblock(lane, 1 - step), low, device(0, 0, 1))
        send((kind, step, -1), which, rblock(lane, step - 1), high, device(0, 0, -1))

    def z_arrive(kind, step):
        which, lane = KINDS[kind]
        low, high = (LOW, HIGH) if step == NZ // 2 else (ALL, ALL)
        arrive((kind, step, 1), which, rblock(lane, -step), low)
        arrive((kind, step, -1), which, rblock(lane, step), high)

    def x_step(step, rows, tag=0):
        low, high = (LOW, HIGH) if step == 2 else (rows, rows)
        send(("x", step, 1, tag), WHOLE, pblock(1 - step, 0), low, device(1, 0, 0))
        send(("x", step, -1, tag), WHOLE, pblock(step - 1, 0), high, device(-1, 0, 0))

    def x_arrive(step, rows, tag=0):
        low, high = (LOW, HIGH) if step == 2 else (rows, rows)
        arrive(("x", step, 1, tag), WHOLE, pblock(-step, 0), low)
        arrive(("x", step, -1, tag), WHOLE, pblock(step, 0), high)

    def y_step(dx, step, rows=ALL, tag=0):
        low, high = (LOW, HIGH) if step == 2 else (rows, rows)
        send(("y", dx, step, 1, tag), WHOLE, pblock(dx, 1 - step), low, device(0, 1, 0))
        send(("y", dx, step, -1, tag), WHOLE, pblock(dx, step - 1), high, device(0, -1, 0))

    def y_arrive(dx, step, rows=ALL, tag=0):
        low, high = (LOW, HIGH) if step == 2 else (rows, rows)
        arrive(("y", dx, step, 1, tag), WHOLE, pblock(dx, -step), low)
        arrive(("y", dx, step, -1, tag), WHOLE, pblock(dx, step), high)

    def cross(step):
        for d in sorted({-step, step} if step < NZ // 2 else {step}):
            send(("cross", d), FEW, rblock(0, d), ALL, device(2, 0, 0))

    def cross_arrive(step):
        for d in sorted({-step, step} if step < NZ // 2 else {step}):
            arrive(("cross", d), FEW, rblock(1, d))

    loads[8].wait()
    for h in range(KVH):
        for g in range(GW):
            column = (h * GW + g) * HD
            scaled = q_ref[:, column : column + HD].T.astype(F32) * SCALE
            high = scaled.astype(BF16)
            qa[h, 0:HD, g * ROWS : (g + 1) * ROWS] = high
            qa[h, HD : 2 * HD, g * ROWS : (g + 1) * ROWS] = (scaled - high.astype(F32)).astype(BF16)
    for load in loads[:8] + loads[9:]:
        load.wait()

    pl.semaphore_wait(barrier, len(peers))

    slots = {0: 0, -1: 1, 1: 2, -2: 3, 2: 4, -3: 5, 3: 6, 4: 7}

    def slot(d):
        return (slots[d] * PIECE, PIECE)

    for d in (1, -1, 2, -2, 3, -3, 4):
        send(("piece", d), WHOLE, own_prompt, slot(0), device(0, 0, d), there=slot(-d if d < 4 else 4))
    send("most", MOST_OF, own_block, ALL, device(2, 0, 0))
    cross(0)
    z_step("few", 1)
    z_step("own", 1)

    bias[0] = jnp.zeros((ROWS, ROWS), F32)

    def set_bias(block, _):
        bias[block + 1] = block_bias(order_ref, len_ref, seq, block)
        return 0

    lax.fori_loop(0, 2 * NZ, set_bias, 0)
    acc[...] = jnp.zeros_like(acc)

    def pieces_arrive(distances):
        for d in distances:
            arrive(("piece", d), WHOLE, own_prompt, slot(-d if d < 4 else 4))

    def event_0():
        pieces_arrive((1, -1, 2, -2))
        y_step(0, 1, NEAR, 0)
        x_step(1, NEAR, 0)
        pieces_arrive((3, -3, 4))
        y_step(0, 1, FAR, 1)
        x_step(1, FAR, 1)

    def event_1():
        z_arrive("few", 1)
        z_step("few", 2)
        cross(1)
        arrive("most", MOST_OF, rblock(1, 0))
        z_step("other", 1)
        y_arrive(0, 1, NEAR, 0)
        y_arrive(0, 1, FAR, 1)
        y_step(0, 2)

    def event_2():
        z_arrive("own", 1)
        z_step("own", 2)
        x_arrive(1, NEAR, 0)
        x_arrive(1, FAR, 1)
        x_step(2, ALL)
        y_step(1, 1)
        y_step(-1, 1)
        z_arrive("few", 2)
        z_step("few", 3)
        cross(2)

    def event_3():
        pass

    def event_4():
        cross_arrive(0)
        y_arrive(0, 2)

    def event_5():
        z_arrive("other", 1)
        z_step("other", 2)
        cross_arrive(1)

    def event_6():
        x_arrive(2, ALL)
        y_step(2, 1)
        z_arrive("own", 2)
        z_step("own", 3)

    def event_7():
        y_arrive(1, 1)
        y_step(1, 2)
        z_arrive("few", 3)
        z_step("few", 4)
        cross(3)

    def event_8():
        z_arrive("other", 2)
        z_step("other", 3)
        cross_arrive(2)

    def event_9():
        y_arrive(-1, 1)
        y_step(-1, 2)

    def event_10():
        z_arrive("own", 3)
        z_step("own", 4)

    def event_11():
        z_arrive("few", 4)
        cross(4)
        y_arrive(2, 1)
        y_step(2, 2)

    def event_12():
        z_arrive("other", 3)
        z_step("other", 4)
        cross_arrive(3)

    def event_13():
        y_arrive(1, 2)
        y_arrive(-1, 2)

    def event_14():
        z_arrive("own", 4)
        z_arrive("other", 4)
        cross_arrive(4)

    def event_15():
        y_arrive(2, 2)

    units = [
        (event_0, own_block, own_prompt),
        (event_1, pblock(0, -1), pblock(0, 1)),
        (event_2, rblock(0, -1), rblock(0, 1)),
        (event_3, pblock(1, 0), pblock(-1, 0)),
        (event_4, rblock(1, 0), pblock(0, 2)),
        (event_5, rblock(1, -1), rblock(1, 1)),
        (event_6, rblock(0, -2), rblock(0, 2)),
        (event_7, pblock(1, -1), pblock(1, 1)),
        (event_8, rblock(1, -2), rblock(1, 2)),
        (event_9, pblock(-1, -1), pblock(-1, 1)),
        (event_10, rblock(0, -3), rblock(0, 3)),
        (event_11, pblock(2, -1), pblock(2, 1)),
        (event_12, rblock(1, -3), rblock(1, 3)),
        (event_13, pblock(1, 2), pblock(-1, 2)),
        (event_14, rblock(0, 4), rblock(1, 4)),
        (event_15, pblock(2, 0), pblock(2, 2)),
    ]
    ones = jnp.ones((16, 2 * ROWS), BF16)

    def keep(unit, block, which):
        return pltpu.make_async_copy(kv.at[:, block], kept_ref.at[:, block], keep_sem.at[2 * unit + which])

    def pick(t, which):
        block = units[0][which]
        for i, unit in enumerate(units):
            block = jnp.where(t == i, unit[which], block)
        return block

    def work(t, _):
        for i, unit in enumerate(units):
            pl.when(t == i)(unit[0])
        one, two = pick(t, 1), pick(t, 2)
        keep(t, one, 0).start()
        keep(t, two, 1).start()
        bias_one = bias.at[jnp.maximum(one - (NPB - 1), 0)]
        bias_two = bias.at[jnp.maximum(two - (NPB - 1), 0)]

        def scores(h):
            part, columns = h // 2, slice(h % 2 * HD, (h % 2 + 1) * HD)
            k = jnp.concatenate([kv[part, one, :, columns], kv[part, two, :, columns]], axis=0)
            return jnp.dot(jnp.concatenate([k, k], axis=1), qa[h], preferred_element_type=F32)

        def weights(s):
            b = jnp.concatenate([bias_one[...], bias_two[...]], axis=0)
            s = jnp.concatenate([s[:, g * ROWS : (g + 1) * ROWS] + b for g in range(GW)], axis=1)
            return jnp.exp2(s).astype(BF16)

        def mix(h, p):
            part, columns = 2 + h // 2, slice(h % 2 * HD, (h % 2 + 1) * HD)
            v = jnp.concatenate([kv[part, one, :, columns].T, kv[part, two, :, columns].T], axis=1)
            acc[h] += jnp.dot(jnp.concatenate([v, ones], axis=0), p, preferred_element_type=F32)

        s, p = {0: scores(0)}, {}
        for h in range(KVH + 1):
            if h + 1 < KVH:
                s[h + 1] = scores(h + 1)
            if h >= 1:
                mix(h - 1, p.pop(h - 1))
            if h < KVH:
                p[h] = weights(s.pop(h))
        return 0

    lax.fori_loop(0, len(units), work, 0)

    scale_row = row_scale(order_ref, len_ref, tags_ref, weight_ref, seq)
    bad = jnp.zeros((1, ROWS), F32)
    for h in range(KVH):
        for g in range(GW):
            columns = slice(g * ROWS, (g + 1) * ROWS)
            total = acc[h, HD : HD + 1, columns]
            bad = jnp.where((total >= LEAST) & (total <= MOST), bad, 1.0)
            mixed = (acc[h, 0:HD, columns] * (scale_row / total)).astype(BF16)
            column = (h * GW + g) * HD
            out_ref[:, column : column + HD] = mixed.T
    bad_ref[...] = bad

    for t, unit in enumerate(units):
        keep(t, unit[1], 0).wait()
        keep(t, unit[2], 1).wait()
    for name, (which, rows) in sent.items():
        here = piece_of(which, own_block, rows)
        copy(name, (here, here), device(0, 0, 1)).wait_send()


def check_rows(len_ref, order_ref, tags_ref, weight_ref, bad_ref, q_ref, kept_ref, first_ref, out_ref, q, kv, out, sem, pass_sem):
    seq = lax.axis_index("seq")
    parts = [slice(i * ROWS // PARTS, (i + 1) * ROWS // PARTS) for i in range(PARTS)]
    into = [pltpu.make_async_copy(first_ref.at[p], out.at[p], pass_sem.at[0, i]) for i, p in enumerate(parts)]
    onto = [pltpu.make_async_copy(out.at[p], out_ref.at[p], pass_sem.at[1, i]) for i, p in enumerate(parts)]
    for load in into:
        load.start()
    for load, store in zip(into, onto):
        load.wait()
        store.start()
    bad = jnp.max(bad_ref[...])
    for store in onto:
        store.wait()

    @pl.when(bad > 0.0)
    def redo():
        for src, dst in ((q_ref, q), (kept_ref, kv)):
            fetch = pltpu.make_async_copy(src, dst, sem)
            fetch.start()
            fetch.wait()
        scale_row = row_scale(order_ref, len_ref, tags_ref, weight_ref, seq)

        def head(index, _):
            columns = pl.ds(pl.multiple_of(index * HD, HD), HD)
            kv_head = lax.div(index, GW)
            part = lax.div(kv_head, 2)
            kv_columns = pl.ds(pl.multiple_of(lax.rem(kv_head, 2) * HD, HD), HD)
            queries = q[:, columns]

            def scores(block):
                s = lax.dot_general(
                    kv[part, block, :, kv_columns], queries, (((1,), (1,)), ((), ())), preferred_element_type=F32
                )
                b = block_bias(order_ref, len_ref, seq, jnp.maximum(block - NPB, 0))
                return jnp.where(block < NPB, s * SCALE, s * SCALE + b)

            def top_of(block, top):
                return jnp.maximum(top, jnp.max(scores(block), axis=0, keepdims=True))

            blocks = kv.shape[1]
            top = lax.fori_loop(0, blocks, top_of, jnp.full((1, ROWS), -jnp.inf, F32))

            def add(block, carry):
                total, mixed = carry
                w = jnp.exp2(scores(block) - top)
                total += jnp.sum(w, axis=0, keepdims=True)
                mixed += jnp.dot(kv[2 + part, block, :, kv_columns].T, w.astype(BF16), preferred_element_type=F32)
                return total, mixed

            total, mixed = lax.fori_loop(
                0, blocks, add, (jnp.zeros((1, ROWS), F32), jnp.zeros((HD, ROWS), F32))
            )
            out[:, columns] = (mixed * (scale_row / total)).astype(BF16).T
            return 0

        lax.fori_loop(0, H, head, 0)
        store = pltpu.make_async_copy(out, out_ref, sem)
        store.start()
        store.wait()


def shards(resp_q, resp_kv, prompt_kv, resp_len, block_order, tags, ver_weight):
    blocks = NPB + 2 * NZ
    smem = pl.BlockSpec(memory_space=pltpu.SMEM)
    vmem = pl.BlockSpec(memory_space=pltpu.VMEM)
    hbm = pl.BlockSpec(memory_space=pltpu.HBM)
    scalars = (resp_len, block_order, tags, ver_weight)
    queries = resp_q[0]
    kv_shape = (4, blocks, ROWS, PART)
    keys = blocks * ROWS
    attended, bad, kept = pl.pallas_call(
        gather_attend,
        out_shape=(
            jax.ShapeDtypeStruct((ROWS, H * HD), BF16),
            jax.ShapeDtypeStruct((1, ROWS), F32),
            jax.ShapeDtypeStruct(kv_shape, BF16),
        ),
        in_specs=[hbm] * 7,
        out_specs=(vmem, vmem, hbm),
        scratch_shapes=[pltpu.SMEM(a.shape, a.dtype) for a in scalars]
        + [
            pltpu.VMEM((ROWS, H * HD), BF16),
            pltpu.VMEM(kv_shape, BF16),
            pltpu.VMEM((KVH, 2 * HD, GW * ROWS), BF16),
            pltpu.VMEM((KVH, HD + 16, GW * ROWS), F32),
            pltpu.VMEM((2 * NZ + 1, ROWS, ROWS), F32),
            pltpu.SemaphoreType.DMA((13,)),
            pltpu.SemaphoreType.DMA((N_MSG,)),
            pltpu.SemaphoreType.DMA((N_MSG,)),
            pltpu.SemaphoreType.DMA((blocks,)),
        ],
        compiler_params=pltpu.CompilerParams(
            collective_id=0, has_side_effects=True, vmem_limit_bytes=60 * 2**20
        ),
        cost_estimate=pl.CostEstimate(
            flops=4 * ROWS * H * HD * keys, bytes_accessed=4 * keys * HALF, transcendentals=ROWS * H * keys
        ),
    )(*scalars, queries, resp_kv[0], prompt_kv)
    final = pl.pallas_call(
        check_rows,
        out_shape=jax.ShapeDtypeStruct((ROWS, H * HD), BF16),
        in_specs=[smem] * 4 + [vmem] + [hbm] * 2 + [pl.BlockSpec(memory_space=pl.ANY)],
        out_specs=hbm,
        scratch_shapes=[
            pltpu.VMEM((ROWS, H * HD), BF16),
            pltpu.VMEM(kv_shape, BF16),
            pltpu.VMEM((ROWS, H * HD), BF16),
            pltpu.SemaphoreType.DMA,
            pltpu.SemaphoreType.DMA((2, PARTS)),
        ],
        compiler_params=pltpu.CompilerParams(vmem_limit_bytes=60 * 2**20),
    )(*scalars, bad, queries, kept, attended)
    return final[None]


def solution(mesh):
    in_specs = (
        P(("grp", "smp"), "seq", None),
        P(("grp", "smp"), "seq", None),
        P(("grp", "smp", "seq"), None),
        P(("grp", "smp")),
        P("grp"),
        P(("grp", "smp"), "seq"),
        P(),
    )
    out_specs = P(("grp", "smp"), "seq", None)
    return jax.shard_map(shards, mesh=mesh, in_specs=in_specs, out_specs=out_specs, check_vma=False)
```

time: 566 us -> 560 us (0.989)
  local copies, waits for them, and re-layouts: 9.24 us -> 0 us
    unnamed x15 -> x0, local copies, waits for them, and re-layouts: 9.24 us -> none
    pallas_call x1, Pallas kernels: 496 us -> 503 us  [shards(): pl.pallas_call(check_rows, out_shape=jax.ShapeDtypeStruct((ROWS, H * HD),...]
where the time goes in v2:
time: 560 us; the launch traced here: 559 us
  Pallas kernels  558 us (100%)
    pallas_call x1, Pallas kernels, shards(): pl.pallas_call(check_rows, out_shape=jax.ShapeDtypeStruct((ROWS, H * HD),...  503 us
    pallas_call x1, Pallas kernels, shards(): pl.pallas_call(gather_attend, out_shape=(jax.ShapeDtypeStruct((ROWS, H *...  55.1 us

profile of v2, /device:TPU:0, one launch (start us, length us, event | category | flops | bytes accessed | tf_op | source)
XLA Modules:
  0.0 558.8 jit_solution(9916749837597310063)
XLA Ops:
  0.7 55.1 %shard_map.73 = (bf16[128,4096]{1,0:T(8,128)(2,1)}, f32[1,128]{1,0:T(1,128)}, bf16[4,32,128,256]{3,2,1,0:T(8,128)(2,1)}) custom-call(s32[1]{0:T(128)S(6)} %copy.8.len_in.len_ref, s32[32]{0:T(128)} %order_ref.1, s32[1,2]{1,0:T(1,128)} %tags_ref.1, f32[4]{0:T(128)} %weight_ref.1, bf16[128,4096]{1,0:T(8,128)(2,1)} %bitcast.3, bf16[128,1024]{1,0:T(8,128)(2,1)} %bitcast.5, ...), custom_call_target="tpu_custom_call" | custom-call | flops 8589934592 | bytes 8388608 | tf_op jit(solution)/shard_map/pallas_call | solution.py:451
  55.8 503.0 %shard_map.74 = bf16[128,4096]{1,0:T(8,128)(2,1)} custom-call(s32[1]{0:T(128)S(6)} %copy.8.len_in.len_ref, s32[32]{0:T(128)} %order_ref.1, s32[1,2]{1,0:T(1,128)} %tags_ref.1, f32[4]{0:T(128)} %weight_ref.1, f32[1,128]{1,0:T(1,128)} %get-tuple-element.8.bad_ref, bf16[128,4096]{1,0:T(8,128)(2,1)} %bitcast.4, ...), custom_call_target="tpu_custom_call" | custom-call | tf_op jit(solution)/shard_map/pallas_call | solution.py:479

commit v3 on v2

--- a/solution.py
+++ b/solution.py
@@ -24,13 +24,13 @@
 LEAST, MOST = 2.0**-80, 2.0**100
 
 PIECE = 16
-PART = 256
-WHOLE, FEW, MOST_OF = slice(0, 4), slice(0, 1), slice(1, 4)
+PARTS = 2 * KVH
+WHOLE, FEW, MOST_OF = slice(0, PARTS), slice(0, 3), slice(3, PARTS)
 KINDS = {"few": (FEW, 0), "own": (MOST_OF, 0), "other": (MOST_OF, 1)}
 ALL, LOW, HIGH = (0, ROWS), (0, ROWS // 2), (ROWS // 2, ROWS // 2)
 NEAR, FAR = (0, 5 * PIECE), (5 * PIECE, 3 * PIECE)
-N_MSG = 64
-PARTS = 4
+N_MSG = 80
+N_PASS = 8
 
 
 def positions(order_ref, block, along, shape):
@@ -63,9 +63,9 @@
 
 def gather_attend(
     len_in, order_in, tags_in, weight_in, q_in, own_in, piece_in,
-    out_ref, bad_ref, kept_ref,
+    out_hbm, bad_ref, kept_ref,
     len_ref, order_ref, tags_ref, weight_ref, q_ref,
-    kv, qa, acc, bias, load_sem, send_sem, recv_sem, keep_sem,
+    out_ref, kv, qa, acc, bias, load_sem, send_sem, recv_sem, keep_sem,
 ):
     grp, smp, seq = lax.axis_index("grp"), lax.axis_index("smp"), lax.axis_index("seq")
     x_hi, z = lax.div(seq, NZ), lax.rem(seq, NZ)
@@ -90,8 +90,8 @@
         pl.semaphore_signal(barrier, inc=1, device_id=peer, device_id_type=MESH)
 
     own_block, own_prompt = rblock(0, 0), pblock(0, 0)
-    pairs = [(piece_in.at[:, k * PART : (k + 1) * PART], kv.at[k, own_prompt, 0:PIECE, :]) for k in range(4)]
-    pairs += [(own_in.at[:, k * PART : (k + 1) * PART], kv.at[k, own_block]) for k in range(4)]
+    pairs = [(piece_in.at[:, k * HD : (k + 1) * HD], kv.at[k, own_prompt, 0:PIECE, :]) for k in range(PARTS)]
+    pairs += [(own_in.at[:, k * HD : (k + 1) * HD], kv.at[k, own_block]) for k in range(PARTS)]
     pairs += [(q_in, q_ref), (len_in, len_ref), (order_in, order_ref), (tags_in, tags_ref), (weight_in, weight_ref)]
     loads = [pltpu.make_async_copy(src, dst, load_sem.at[i]) for i, (src, dst) in enumerate(pairs)]
     for load in loads:
@@ -146,15 +146,21 @@
         arrive(("x", step, 1, tag), WHOLE, pblock(-step, 0), low)
         arrive(("x", step, -1, tag), WHOLE, pblock(step, 0), high)
 
-    def y_step(dx, step, rows=ALL, tag=0):
-        low, high = (LOW, HIGH) if step == 2 else (rows, rows)
-        send(("y", dx, step, 1, tag), WHOLE, pblock(dx, 1 - step), low, device(0, 1, 0))
-        send(("y", dx, step, -1, tag), WHOLE, pblock(dx, step - 1), high, device(0, -1, 0))
-
-    def y_arrive(dx, step, rows=ALL, tag=0):
-        low, high = (LOW, HIGH) if step == 2 else (rows, rows)
-        arrive(("y", dx, step, 1, tag), WHOLE, pblock(dx, -step), low)
-        arrive(("y", dx, step, -1, tag), WHOLE, pblock(dx, step), high)
+    def y_step(dx, step, right=ALL, left=ALL, tag=0):
+        send(("y", dx, step, 1, tag), WHOLE, pblock(dx, 1 - step), right, device(0, 1, 0))
+        send(("y", dx, step, -1, tag), WHOLE, pblock(dx, step - 1), left, device(0, -1, 0))
+
+    def y_arrive(dx, step, right=ALL, left=ALL, tag=0):
+        arrive(("y", dx, step, 1, tag), WHOLE, pblock(dx, -step), right)
+        arrive(("y", dx, step, -1, tag), WHOLE, pblock(dx, step), left)
+
+    def far_step():
+        for d in (1, -1):
+            send(("far", d), WHOLE, pblock(0, 2), ALL, device(d, 0, 0))
+
+    def far_arrive():
+        for d in (1, -1):
+            arrive(("far", d), WHOLE, pblock(-d, 2))
 
     def cross(step):
         for d in sorted({-step, step} if step < NZ // 2 else {step}):
@@ -164,7 +170,31 @@
         for d in sorted({-step, step} if step < NZ // 2 else {step}):
             arrive(("cross", d), FEW, rblock(1, d))
 
-    loads[8].wait()
+    for load in loads:
+        load.wait()
+    bias[0] = jnp.zeros((ROWS, ROWS), F32)
+
+    def set_bias(block, _):
+        bias[block + 1] = block_bias(order_ref, len_ref, seq, block)
+        return 0
+
+    lax.fori_loop(0, 2 * NZ, set_bias, 0)
+    acc[...] = jnp.zeros_like(acc)
+
+    pl.semaphore_wait(barrier, len(peers))
+
+    slots = {0: 0, -1: 1, 1: 2, -2: 3, 2: 4, -3: 5, 3: 6, 4: 7}
+
+    def slot(d):
+        return (slots[d] * PIECE, PIECE)
+
+    for d in (1, -1, 2, -2, 3, -3, 4):
+        send(("piece", d), WHOLE, own_prompt, slot(0), device(0, 0, d), there=slot(-d if d < 4 else 4))
+    send("most", MOST_OF, own_block, ALL, device(2, 0, 0))
+    cross(0)
+    z_step("few", 1)
+    z_step("own", 1)
+
     for h in range(KVH):
         for g in range(GW):
             column = (h * GW + g) * HD
@@ -172,90 +202,67 @@
             high = scaled.astype(BF16)
             qa[h, 0:HD, g * ROWS : (g + 1) * ROWS] = high
             qa[h, HD : 2 * HD, g * ROWS : (g + 1) * ROWS] = (scaled - high.astype(F32)).astype(BF16)
-    for load in loads[:8] + loads[9:]:
-        load.wait()
-
-    pl.semaphore_wait(barrier, len(peers))
-
-    slots = {0: 0, -1: 1, 1: 2, -2: 3, 2: 4, -3: 5, 3: 6, 4: 7}
-
-    def slot(d):
-        return (slots[d] * PIECE, PIECE)
-
-    for d in (1, -1, 2, -2, 3, -3, 4):
-        send(("piece", d), WHOLE, own_prompt, slot(0), device(0, 0, d), there=slot(-d if d < 4 else 4))
-    send("most", MOST_OF, own_block, ALL, device(2, 0, 0))
-    cross(0)
-    z_step("few", 1)
-    z_step("own", 1)
-
-    bias[0] = jnp.zeros((ROWS, ROWS), F32)
-
-    def set_bias(block, _):
-        bias[block + 1] = block_bias(order_ref, len_ref, seq, block)
-        return 0
-
-    lax.fori_loop(0, 2 * NZ, set_bias, 0)
-    acc[...] = jnp.zeros_like(acc)
-
     def pieces_arrive(distances):
         for d in distances:
             arrive(("piece", d), WHOLE, own_prompt, slot(-d if d < 4 else 4))
 
     def event_0():
         pieces_arrive((1, -1, 2, -2))
-        y_step(0, 1, NEAR, 0)
-        x_step(1, NEAR, 0)
-        pieces_arrive((3, -3, 4))
-        y_step(0, 1, FAR, 1)
-        x_step(1, FAR, 1)
-
-    def event_1():
+        y_step(0, 1, NEAR, NEAR)
+        x_step(1, NEAR)
         z_arrive("few", 1)
         z_step("few", 2)
         cross(1)
         arrive("most", MOST_OF, rblock(1, 0))
         z_step("other", 1)
-        y_arrive(0, 1, NEAR, 0)
-        y_arrive(0, 1, FAR, 1)
-        y_step(0, 2)
-
-    def event_2():
+        pieces_arrive((3, -3, 4))
+        y_step(0, 1, FAR, FAR, 1)
+        x_step(1, FAR, 1)
+
+    def event_1():
+        x_arrive(1, NEAR)
+        y_step(1, 1, NEAR, NEAR)
+        y_step(-1, 1, NEAR, NEAR)
         z_arrive("own", 1)
         z_step("own", 2)
-        x_arrive(1, NEAR, 0)
-        x_arrive(1, FAR, 1)
-        x_step(2, ALL)
-        y_step(1, 1)
-        y_step(-1, 1)
+
+    def event_2():
+        y_arrive(0, 1, NEAR, NEAR)
+        y_arrive(0, 1, FAR, FAR, 1)
+        y_step(0, 2, LOW, HIGH)
+
+    def event_3():
         z_arrive("few", 2)
         z_step("few", 3)
         cross(2)
-
-    def event_3():
-        pass
+        x_arrive(1, FAR, 1)
+        x_step(2, ALL)
+        y_step(1, 1, FAR, FAR, 1)
+        y_step(-1, 1, FAR, FAR, 1)
 
     def event_4():
-        cross_arrive(0)
-        y_arrive(0, 2)
-
-    def event_5():
         z_arrive("other", 1)
         z_step("other", 2)
         cross_arrive(1)
 
-    def event_6():
-        x_arrive(2, ALL)
-        y_step(2, 1)
+    def event_5():
         z_arrive("own", 2)
         z_step("own", 3)
 
-    def event_7():
-        y_arrive(1, 1)
-        y_step(1, 2)
+    def event_6():
         z_arrive("few", 3)
         z_step("few", 4)
         cross(3)
+        y_arrive(0, 2, LOW, HIGH)
+        far_step()
+        cross_arrive(0)
+
+    def event_7():
+        x_arrive(2, ALL)
+        y_step(2, 1, LOW, HIGH)
+        y_step(2, 1, HIGH, LOW, 1)
+        y_arrive(-1, 1, NEAR, NEAR)
+        y_arrive(-1, 1, FAR, FAR, 1)
 
     def event_8():
         z_arrive("other", 2)
@@ -263,8 +270,8 @@
         cross_arrive(2)
 
     def event_9():
-        y_arrive(-1, 1)
-        y_step(-1, 2)
+        y_arrive(1, 1, NEAR, NEAR)
+        y_arrive(1, 1, FAR, FAR, 1)
 
     def event_10():
         z_arrive("own", 3)
@@ -273,8 +280,9 @@
     def event_11():
         z_arrive("few", 4)
         cross(4)
-        y_arrive(2, 1)
-        y_step(2, 2)
+        y_arrive(2, 1, LOW, HIGH)
+        y_step(2, 2, LOW, HIGH)
+        y_arrive(2, 1, HIGH, LOW, 1)
 
     def event_12():
         z_arrive("other", 3)
@@ -282,34 +290,33 @@
         cross_arrive(3)
 
     def event_13():
-        y_arrive(1, 2)
-        y_arrive(-1, 2)
+        far_arrive()
 
     def event_14():
+        y_arrive(2, 2, LOW, HIGH)
+
+    def event_15():
         z_arrive("own", 4)
         z_arrive("other", 4)
         cross_arrive(4)
 
-    def event_15():
-        y_arrive(2, 2)
-
     units = [
         (event_0, own_block, own_prompt),
-        (event_1, pblock(0, -1), pblock(0, 1)),
-        (event_2, rblock(0, -1), rblock(0, 1)),
+        (event_1, rblock(0, -1), rblock(0, 1)),
+        (event_2, pblock(0, -1), pblock(0, 1)),
         (event_3, pblock(1, 0), pblock(-1, 0)),
-        (event_4, rblock(1, 0), pblock(0, 2)),
-        (event_5, rblock(1, -1), rblock(1, 1)),
-        (event_6, rblock(0, -2), rblock(0, 2)),
-        (event_7, pblock(1, -1), pblock(1, 1)),
+        (event_4, rblock(1, -1), rblock(1, 1)),
+        (event_5, rblock(0, -2), rblock(0, 2)),
+        (event_6, rblock(1, 0), pblock(0, 2)),
+        (event_7, pblock(-1, -1), pblock(-1, 1)),
         (event_8, rblock(1, -2), rblock(1, 2)),
-        (event_9, pblock(-1, -1), pblock(-1, 1)),
+        (event_9, pblock(1, -1), pblock(1, 1)),
         (event_10, rblock(0, -3), rblock(0, 3)),
         (event_11, pblock(2, -1), pblock(2, 1)),
         (event_12, rblock(1, -3), rblock(1, 3)),
         (event_13, pblock(1, 2), pblock(-1, 2)),
-        (event_14, rblock(0, 4), rblock(1, 4)),
-        (event_15, pblock(2, 0), pblock(2, 2)),
+        (event_14, pblock(2, 0), pblock(2, 2)),
+        (event_15, rblock(0, 4), rblock(1, 4)),
     ]
     ones = jnp.ones((16, 2 * ROWS), BF16)
 
@@ -332,8 +339,7 @@
         bias_two = bias.at[jnp.maximum(two - (NPB - 1), 0)]
 
         def scores(h):
-            part, columns = h // 2, slice(h % 2 * HD, (h % 2 + 1) * HD)
-            k = jnp.concatenate([kv[part, one, :, columns], kv[part, two, :, columns]], axis=0)
+            k = jnp.concatenate([kv[h, one], kv[h, two]], axis=0)
             return jnp.dot(jnp.concatenate([k, k], axis=1), qa[h], preferred_element_type=F32)
 
         def weights(s):
@@ -342,8 +348,7 @@
             return jnp.exp2(s).astype(BF16)
 
         def mix(h, p):
-            part, columns = 2 + h // 2, slice(h % 2 * HD, (h % 2 + 1) * HD)
-            v = jnp.concatenate([kv[part, one, :, columns].T, kv[part, two, :, columns].T], axis=1)
+            v = jnp.concatenate([kv[KVH + h, one].T, kv[KVH + h, two].T], axis=1)
             acc[h] += jnp.dot(jnp.concatenate([v, ones], axis=0), p, preferred_element_type=F32)
 
         s, p = {0: scores(0)}, {}
@@ -360,6 +365,8 @@
 
     scale_row = row_scale(order_ref, len_ref, tags_ref, weight_ref, seq)
     bad = jnp.zeros((1, ROWS), F32)
+    spans = [slice(h * GW * HD, (h + 1) * GW * HD) for h in range(KVH)]
+    stores = [pltpu.make_async_copy(out_ref.at[:, c], out_hbm.at[:, c], load_sem.at[i]) for i, c in enumerate(spans)]
     for h in range(KVH):
         for g in range(GW):
             columns = slice(g * ROWS, (g + 1) * ROWS)
@@ -368,8 +375,11 @@
             mixed = (acc[h, 0:HD, columns] * (scale_row / total)).astype(BF16)
             column = (h * GW + g) * HD
             out_ref[:, column : column + HD] = mixed.T
+        stores[h].start()
     bad_ref[...] = bad
 
+    for store in stores:
+        store.wait()
     for t, unit in enumerate(units):
         keep(t, unit[1], 0).wait()
         keep(t, unit[2], 1).wait()
@@ -378,9 +388,13 @@
         copy(name, (here, here), device(0, 0, 1)).wait_send()
 
 
-def check_rows(len_ref, order_ref, tags_ref, weight_ref, bad_ref, q_ref, kept_ref, first_ref, out_ref, q, kv, out, sem, pass_sem):
+def check_rows(
+    len_in, order_in, tags_in, weight_in, bad_ref, q_ref, kept_ref, first_ref,
+    out_ref,
+    len_ref, order_ref, tags_ref, weight_ref, q, kv, out, sem, pass_sem,
+):
     seq = lax.axis_index("seq")
-    parts = [slice(i * ROWS // PARTS, (i + 1) * ROWS // PARTS) for i in range(PARTS)]
+    parts = [slice(i * ROWS // N_PASS, (i + 1) * ROWS // N_PASS) for i in range(N_PASS)]
     into = [pltpu.make_async_copy(first_ref.at[p], out.at[p], pass_sem.at[0, i]) for i, p in enumerate(parts)]
     onto = [pltpu.make_async_copy(out.at[p], out_ref.at[p], pass_sem.at[1, i]) for i, p in enumerate(parts)]
     for load in into:
@@ -394,7 +408,8 @@
 
     @pl.when(bad > 0.0)
     def redo():
-        for src, dst in ((q_ref, q), (kept_ref, kv)):
+        scalars = ((len_in, len_ref), (order_in, order_ref), (tags_in, tags_ref), (weight_in, weight_ref))
+        for src, dst in ((q_ref, q), (kept_ref, kv), *scalars):
             fetch = pltpu.make_async_copy(src, dst, sem)
             fetch.start()
             fetch.wait()
@@ -403,13 +418,11 @@
         def head(index, _):
             columns = pl.ds(pl.multiple_of(index * HD, HD), HD)
             kv_head = lax.div(index, GW)
-            part = lax.div(kv_head, 2)
-            kv_columns = pl.ds(pl.multiple_of(lax.rem(kv_head, 2) * HD, HD), HD)
             queries = q[:, columns]
 
             def scores(block):
                 s = lax.dot_general(
-                    kv[part, block, :, kv_columns], queries, (((1,), (1,)), ((), ())), preferred_element_type=F32
+                    kv[kv_head, block], queries, (((1,), (1,)), ((), ())), preferred_element_type=F32
                 )
                 b = block_bias(order_ref, len_ref, seq, jnp.maximum(block - NPB, 0))
                 return jnp.where(block < NPB, s * SCALE, s * SCALE + b)
@@ -424,7 +437,7 @@
                 total, mixed = carry
                 w = jnp.exp2(scores(block) - top)
                 total += jnp.sum(w, axis=0, keepdims=True)
-                mixed += jnp.dot(kv[2 + part, block, :, kv_columns].T, w.astype(BF16), preferred_element_type=F32)
+                mixed += jnp.dot(kv[KVH + kv_head, block].T, w.astype(BF16), preferred_element_type=F32)
                 return total, mixed
 
             total, mixed = lax.fori_loop(
@@ -441,12 +454,11 @@
 
 def shards(resp_q, resp_kv, prompt_kv, resp_len, block_order, tags, ver_weight):
     blocks = NPB + 2 * NZ
-    smem = pl.BlockSpec(memory_space=pltpu.SMEM)
     vmem = pl.BlockSpec(memory_space=pltpu.VMEM)
     hbm = pl.BlockSpec(memory_space=pltpu.HBM)
     scalars = (resp_len, block_order, tags, ver_weight)
     queries = resp_q[0]
-    kv_shape = (4, blocks, ROWS, PART)
+    kv_shape = (PARTS, blocks, ROWS, HD)
     keys = blocks * ROWS
     attended, bad, kept = pl.pallas_call(
         gather_attend,
@@ -456,15 +468,16 @@
             jax.ShapeDtypeStruct(kv_shape, BF16),
         ),
         in_specs=[hbm] * 7,
-        out_specs=(vmem, vmem, hbm),
+        out_specs=(hbm, vmem, hbm),
         scratch_shapes=[pltpu.SMEM(a.shape, a.dtype) for a in scalars]
         + [
+            pltpu.VMEM((ROWS, H * HD), BF16),
             pltpu.VMEM((ROWS, H * HD), BF16),
             pltpu.VMEM(kv_shape, BF16),
             pltpu.VMEM((KVH, 2 * HD, GW * ROWS), BF16),
             pltpu.VMEM((KVH, HD + 16, GW * ROWS), F32),
             pltpu.VMEM((2 * NZ + 1, ROWS, ROWS), F32),
-            pltpu.SemaphoreType.DMA((13,)),
+            pltpu.SemaphoreType.DMA((2 * PARTS + 5,)),
             pltpu.SemaphoreType.DMA((N_MSG,)),
             pltpu.SemaphoreType.DMA((N_MSG,)),
             pltpu.SemaphoreType.DMA((blocks,)),
@@ -479,14 +492,15 @@
     final = pl.pallas_call(
         check_rows,
         out_shape=jax.ShapeDtypeStruct((ROWS, H * HD), BF16),
-        in_specs=[smem] * 4 + [vmem] + [hbm] * 2 + [pl.BlockSpec(memory_space=pl.ANY)],
+        in_specs=[hbm] * 4 + [vmem] + [hbm] * 3,
         out_specs=hbm,
-        scratch_shapes=[
+        scratch_shapes=[pltpu.SMEM(a.shape, a.dtype) for a in scalars]
+        + [
             pltpu.VMEM((ROWS, H * HD), BF16),
             pltpu.VMEM(kv_shape, BF16),
             pltpu.VMEM((ROWS, H * HD), BF16),
             pltpu.SemaphoreType.DMA,
-            pltpu.SemaphoreType.DMA((2, PARTS)),
+            pltpu.SemaphoreType.DMA((2, N_PASS)),
         ],
         compiler_params=pltpu.CompilerParams(vmem_limit_bytes=60 * 2**20),
     )(*scalars, bad, queries, kept, attended)

time: 560 us -> 560 us (level)
  no operation moved by 1% of the time
where the time goes in v3:
time: 560 us; the launch traced here: 559 us
  Pallas kernels  558 us (100%)
    pallas_call x1, Pallas kernels, shards(): pl.pallas_call(check_rows, out_shape=jax.ShapeDtypeStruct((ROWS, H * HD),...  506 us
    pallas_call x1, Pallas kernels, shards(): pl.pallas_call(gather_attend, out_shape=(jax.ShapeDtypeStruct((ROWS, H *...  52.2 us

profile of v3, /device:TPU:0, one launch (start us, length us, event | category | flops | bytes accessed | tf_op | source)
XLA Modules:
  0.0 558.5 jit_solution(9809038220241602645)
XLA Ops:
  0.7 52.2 %shard_map.73 = (bf16[128,4096]{1,0:T(8,128)(2,1)}, f32[1,128]{1,0:T(1,128)}, bf16[8,32,128,128]{3,2,1,0:T(8,128)(2,1)}) custom-call(s32[1]{0:T(128)S(6)} %copy.8.len_in, s32[32]{0:T(128)} %order_in.3, s32[1,2]{1,0:T(1,128)} %tags_in.3, f32[4]{0:T(128)} %weight_in.3, bf16[128,4096]{1,0:T(8,128)(2,1)} %bitcast.3, bf16[128,1024]{1,0:T(8,128)(2,1)} %bitcast.5, ...), custom_call_target="tpu_custom_call" | custom-call | flops 8589934592 | bytes 8388608 | tf_op jit(solution)/shard_map/pallas_call | solution.py:463
  52.9 505.7 %shard_map.74 = bf16[128,4096]{1,0:T(8,128)(2,1)} custom-call(s32[1]{0:T(128)S(6)} %copy.8.len_in, s32[32]{0:T(128)} %order_in.3, s32[1,2]{1,0:T(1,128)} %tags_in.3, f32[4]{0:T(128)} %weight_in.3, f32[1,128]{1,0:T(1,128)} %get-tuple-element.8.bad_ref, bf16[128,4096]{1,0:T(8,128)(2,1)} %bitcast.4, bf16[8,32,128,128]{3,2,1,0:T(8,128)(2,1)} %get-tuple-element.9.kept_ref, ...), custom_call_target="tpu_custom_call" | custom-call | tf_op jit(solution)/shard_map/pallas_call | solution.py:492

commit v4 on v3

--- a/solution.py
+++ b/solution.py
@@ -389,19 +389,22 @@
 
 
 def check_rows(
-    len_in, order_in, tags_in, weight_in, bad_ref, q_ref, kept_ref, first_ref,
+    len_in, order_in, tags_in, weight_in, bad_in, q_ref, kept_ref, first_ref,
     out_ref,
-    len_ref, order_ref, tags_ref, weight_ref, q, kv, out, sem, pass_sem,
+    len_ref, order_ref, tags_ref, weight_ref, bad_ref, q, kv, out, sem, pass_sem,
 ):
     seq = lax.axis_index("seq")
     parts = [slice(i * ROWS // N_PASS, (i + 1) * ROWS // N_PASS) for i in range(N_PASS)]
     into = [pltpu.make_async_copy(first_ref.at[p], out.at[p], pass_sem.at[0, i]) for i, p in enumerate(parts)]
     onto = [pltpu.make_async_copy(out.at[p], out_ref.at[p], pass_sem.at[1, i]) for i, p in enumerate(parts)]
+    flag = pltpu.make_async_copy(bad_in, bad_ref, sem)
     for load in into:
         load.start()
+    flag.start()
     for load, store in zip(into, onto):
         load.wait()
         store.start()
+    flag.wait()
     bad = jnp.max(bad_ref[...])
     for store in onto:
         store.wait()
@@ -492,10 +495,11 @@
     final = pl.pallas_call(
         check_rows,
         out_shape=jax.ShapeDtypeStruct((ROWS, H * HD), BF16),
-        in_specs=[hbm] * 4 + [vmem] + [hbm] * 3,
+        in_specs=[hbm] * 8,
         out_specs=hbm,
         scratch_shapes=[pltpu.SMEM(a.shape, a.dtype) for a in scalars]
         + [
+            pltpu.VMEM((1, ROWS), F32),
             pltpu.VMEM((ROWS, H * HD), BF16),
             pltpu.VMEM(kv_shape, BF16),
             pltpu.VMEM((ROWS, H * HD), BF16),

time: 560 us -> 560 us (level)
  no operation moved by 1% of the time
where the time goes in v4:
time: 560 us; the launch traced here: 558 us
  Pallas kernels  557 us (99%)
    pallas_call x1, Pallas kernels, shards(): pl.pallas_call(check_rows, out_shape=jax.ShapeDtypeStruct((ROWS, H * HD),...  505 us
    pallas_call x1, Pallas kernels, shards(): pl.pallas_call(gather_attend, out_shape=(jax.ShapeDtypeStruct((ROWS, H *...  52.2 us

profile of v4, /device:TPU:0, one launch (start us, length us, event | category | flops | bytes accessed | tf_op | source)
XLA Modules:
  0.0 557.9 jit_solution(8608843812421192027)
XLA Ops:
  0.7 52.2 %shard_map.73 = (bf16[128,4096]{1,0:T(8,128)(2,1)}, f32[1,128]{1,0:T(1,128)}, bf16[8,32,128,128]{3,2,1,0:T(8,128)(2,1)}) custom-call(s32[1]{0:T(128)S(6)} %copy.8.len_in, s32[32]{0:T(128)} %order_in.3, s32[1,2]{1,0:T(1,128)} %tags_in.3, f32[4]{0:T(128)} %weight_in.3, bf16[128,4096]{1,0:T(8,128)(2,1)} %bitcast.3, bf16[128,1024]{1,0:T(8,128)(2,1)} %bitcast.5, ...), custom_call_target="tpu_custom_call" | custom-call | flops 8589934592 | bytes 8388608 | tf_op jit(solution)/shard_map/pallas_call | solution.py:466
  52.9 505.0 %shard_map.74 = bf16[128,4096]{1,0:T(8,128)(2,1)} custom-call(s32[1]{0:T(128)S(6)} %copy.8.len_in, s32[32]{0:T(128)} %order_in.3, s32[1,2]{1,0:T(1,128)} %tags_in.3, f32[4]{0:T(128)} %weight_in.3, f32[1,128]{1,0:T(1,128)} %get-tuple-element.8.bad_in, bf16[128,4096]{1,0:T(8,128)(2,1)} %bitcast.4, bf16[8,32,128,128]{3,2,1,0:T(8,128)(2,1)} %get-tuple-element.9.kept_ref, ...), custom_call_target="tpu_custom_call" | custom-call | tf_op jit(solution)/shard_map/pallas_call | solution.py:495

commit v5 on v4

--- a/solution.py
+++ b/solution.py
@@ -329,10 +329,7 @@
             block = jnp.where(t == i, unit[which], block)
         return block
 
-    def work(t, _):
-        for i, unit in enumerate(units):
-            pl.when(t == i)(unit[0])
-        one, two = pick(t, 1), pick(t, 2)
+    def work(t, one, two, finish=None):
         keep(t, one, 0).start()
         keep(t, two, 1).start()
         bias_one = bias.at[jnp.maximum(one - (NPB - 1), 0)]
@@ -357,17 +354,26 @@
                 s[h + 1] = scores(h + 1)
             if h >= 1:
                 mix(h - 1, p.pop(h - 1))
+                if finish is not None:
+                    finish(h - 1)
             if h < KVH:
                 p[h] = weights(s.pop(h))
+
+    def step(t, _):
+        for i, unit in enumerate(units[:-1]):
+            pl.when(t == i)(unit[0])
+        work(t, pick(t, 1), pick(t, 2))
         return 0
 
-    lax.fori_loop(0, len(units), work, 0)
+    lax.fori_loop(0, len(units) - 1, step, 0)
 
     scale_row = row_scale(order_ref, len_ref, tags_ref, weight_ref, seq)
-    bad = jnp.zeros((1, ROWS), F32)
     spans = [slice(h * GW * HD, (h + 1) * GW * HD) for h in range(KVH)]
     stores = [pltpu.make_async_copy(out_ref.at[:, c], out_hbm.at[:, c], load_sem.at[i]) for i, c in enumerate(spans)]
-    for h in range(KVH):
+    bad_ref[...] = jnp.zeros((1, ROWS), F32)
+
+    def finish(h):
+        bad = bad_ref[...]
         for g in range(GW):
             columns = slice(g * ROWS, (g + 1) * ROWS)
             total = acc[h, HD : HD + 1, columns]
@@ -375,8 +381,12 @@
             mixed = (acc[h, 0:HD, columns] * (scale_row / total)).astype(BF16)
             column = (h * GW + g) * HD
             out_ref[:, column : column + HD] = mixed.T
+        bad_ref[...] = bad
         stores[h].start()
-    bad_ref[...] = bad
+
+    last = len(units) - 1
+    units[last][0]()
+    work(last, units[last][1], units[last][2], finish)
 
     for store in stores:
         store.wait()

time: 560 us -> 559 us (level)
  no operation moved by 1% of the time
where the time goes in v5:
time: 559 us; the launch traced here: 558 us
  Pallas kernels  557 us (100%)
    pallas_call x1, Pallas kernels, shards(): pl.pallas_call(check_rows, out_shape=jax.ShapeDtypeStruct((ROWS, H * HD),...  505 us
    pallas_call x1, Pallas kernels, shards(): pl.pallas_call(gather_attend, out_shape=(jax.ShapeDtypeStruct((ROWS, H *...  51.9 us

profile of v5, /device:TPU:0, one launch (start us, length us, event | category | flops | bytes accessed | tf_op | source)
XLA Modules:
  0.0 557.6 jit_solution(1193280925361129906)
XLA Ops:
  0.7 51.9 %shard_map.73 = (bf16[128,4096]{1,0:T(8,128)(2,1)}, f32[1,128]{1,0:T(1,128)}, bf16[8,32,128,128]{3,2,1,0:T(8,128)(2,1)}) custom-call(s32[1]{0:T(128)S(6)} %copy.8.len_in, s32[32]{0:T(128)} %order_in.3, s32[1,2]{1,0:T(1,128)} %tags_in.3, f32[4]{0:T(128)} %weight_in.3, bf16[128,4096]{1,0:T(8,128)(2,1)} %bitcast.3, bf16[128,1024]{1,0:T(8,128)(2,1)} %bitcast.5, ...), custom_call_target="tpu_custom_call" | custom-call | flops 8589934592 | bytes 8388608 | tf_op jit(solution)/shard_map/pallas_call | solution.py:476
  52.6 505.0 %shard_map.74 = bf16[128,4096]{1,0:T(8,128)(2,1)} custom-call(s32[1]{0:T(128)S(6)} %copy.8.len_in, s32[32]{0:T(128)} %order_in.3, s32[1,2]{1,0:T(1,128)} %tags_in.3, f32[4]{0:T(128)} %weight_in.3, f32[1,128]{1,0:T(1,128)} %get-tuple-element.8.bad_in, bf16[128,4096]{1,0:T(8,128)(2,1)} %bitcast.4, bf16[8,32,128,128]{3,2,1,0:T(8,128)(2,1)} %get-tuple-element.9.kept_ref, ...), custom_call_target="tpu_custom_call" | custom-call | tf_op jit(solution)/shard_map/pallas_call | solution.py:505

commit v6 on v5

--- a/solution.py
+++ b/solution.py
@@ -191,7 +191,6 @@
     for d in (1, -1, 2, -2, 3, -3, 4):
         send(("piece", d), WHOLE, own_prompt, slot(0), device(0, 0, d), there=slot(-d if d < 4 else 4))
     send("most", MOST_OF, own_block, ALL, device(2, 0, 0))
-    cross(0)
     z_step("few", 1)
     z_step("own", 1)
 
@@ -212,12 +211,13 @@
         x_step(1, NEAR)
         z_arrive("few", 1)
         z_step("few", 2)
-        cross(1)
         arrive("most", MOST_OF, rblock(1, 0))
         z_step("other", 1)
         pieces_arrive((3, -3, 4))
         y_step(0, 1, FAR, FAR, 1)
         x_step(1, FAR, 1)
+        cross(1)
+        cross(0)
 
     def event_1():
         x_arrive(1, NEAR)
@@ -243,11 +243,11 @@
     def event_4():
         z_arrive("other", 1)
         z_step("other", 2)
-        cross_arrive(1)
-
-    def event_5():
         z_arrive("own", 2)
         z_step("own", 3)
+
+    def event_5():
+        cross_arrive(1)
 
     def event_6():
         z_arrive("few", 3)
@@ -305,8 +305,8 @@
         (event_1, rblock(0, -1), rblock(0, 1)),
         (event_2, pblock(0, -1), pblock(0, 1)),
         (event_3, pblock(1, 0), pblock(-1, 0)),
-        (event_4, rblock(1, -1), rblock(1, 1)),
-        (event_5, rblock(0, -2), rblock(0, 2)),
+        (event_4, rblock(0, -2), rblock(0, 2)),
+        (event_5, rblock(1, -1), rblock(1, 1)),
         (event_6, rblock(1, 0), pblock(0, 2)),
         (event_7, pblock(-1, -1), pblock(-1, 1)),
         (event_8, rblock(1, -2), rblock(1, 2)),

time: 559 us -> 561 us (level)
  no operation moved by 1% of the time
where the time goes in v6:
time: 561 us; the launch traced here: 559 us
  Pallas kernels  559 us (100%)
    pallas_call x1, Pallas kernels, shards(): pl.pallas_call(check_rows, out_shape=jax.ShapeDtypeStruct((ROWS, H * HD),...  505 us
    pallas_call x1, Pallas kernels, shards(): pl.pallas_call(gather_attend, out_shape=(jax.ShapeDtypeStruct((ROWS, H *...  53.7 us

profile of v6, /device:TPU:0, one launch (start us, length us, event | category | flops | bytes accessed | tf_op | source)
XLA Modules:
  0.0 559.3 jit_solution(13020046038801210205)
XLA Ops:
  0.7 53.7 %shard_map.73 = (bf16[128,4096]{1,0:T(8,128)(2,1)}, f32[1,128]{1,0:T(1,128)}, bf16[8,32,128,128]{3,2,1,0:T(8,128)(2,1)}) custom-call(s32[1]{0:T(128)S(6)} %copy.8.len_in, s32[32]{0:T(128)} %order_in.3, s32[1,2]{1,0:T(1,128)} %tags_in.3, f32[4]{0:T(128)} %weight_in.3, bf16[128,4096]{1,0:T(8,128)(2,1)} %bitcast.3, bf16[128,1024]{1,0:T(8,128)(2,1)} %bitcast.5, ...), custom_call_target="tpu_custom_call" | custom-call | flops 8589934592 | bytes 8388608 | tf_op jit(solution)/shard_map/pallas_call | solution.py:476
  54.3 505.0 %shard_map.74 = bf16[128,4096]{1,0:T(8,128)(2,1)} custom-call(s32[1]{0:T(128)S(6)} %copy.8.len_in, s32[32]{0:T(128)} %order_in.3, s32[1,2]{1,0:T(1,128)} %tags_in.3, f32[4]{0:T(128)} %weight_in.3, f32[1,128]{1,0:T(1,128)} %get-tuple-element.8.bad_in, bf16[128,4096]{1,0:T(8,128)(2,1)} %bitcast.4, bf16[8,32,128,128]{3,2,1,0:T(8,128)(2,1)} %get-tuple-element.9.kept_ref, ...), custom_call_target="tpu_custom_call" | custom-call | tf_op jit(solution)/shard_map/pallas_call | solution.py:505
